TPU v7x, 32 devices: a whole 2x2x4 slice. The times are simulated.
32 devices in a mesh: ut: 4 (over z), it: 8 (over y, x, core).
Axes of the slice: x: 2, y: 2, z: 4, core: 2. Of those that a mesh axis runs over, the one named last changes fastest.
Arguments:
- user_emb: float32 [2048, 512], P('ut'), may hold values from -1 to 1
- tag_emb: float32 [1024, 512], P('ut'), may hold values from -1 to 1
- item_emb: float32 [2048, 512], P('it'), may hold values from -1 to 1
- user_tile_block: int32 [128], P(('ut', 'it')), may hold values from 0 to 3
- user_tile_item: int32 [128], P(('ut', 'it')), may hold values from 0 to 1
- user_tile_counts: int32 [128, 128, 128], P(('ut', 'it')), may hold values from 0 to 3
- tag_tile_block: int32 [64], P(('ut', 'it')), may hold values from 0 to 1
- tag_tile_item: int32 [64], P(('ut', 'it')), may hold values from 0 to 1
- tag_tile_counts: int32 [64, 128, 128], P(('ut', 'it')), may hold values from 0 to 3
Outputs:
- item_block: float32 [2048, 128], P('it')
- user_block: float32 [2048, 128], P('ut')
- tag_block: float32 [1024, 128], P('ut')
Inputs may be any that keep to these rules, and one draw needn't show every extreme that they name: `user_tile_block`: A pair of blocks may recur in several tiles of one device; their counts then add. `tag_tile_block`: A pair of blocks may recur in several tiles of one device; their counts then add.
All inputs are finite; a program needn't handle non-finite values.
Results may differ from a plain program's by a relative error of at most 0.0003.
Values sent between devices are 32-bit elements; how exact they have to be, the bound alone decides.
A program may use at most 64 MiB of HBM per device.

v0:
```python
import functools

import jax
import jax.numpy as jnp
from jax import lax
from jax.experimental import pallas as pl
from jax.experimental.pallas import tpu as pltpu
from jax.sharding import PartitionSpec as P

BLK = 128
CG_STEPS = 3


CONFIDENCE = 0.5
UNSEEN_WEIGHT = 0.1
PENALTY = 1.0
EPSILON = 1e-06
EXACT_PRECISION = lax.Precision.HIGHEST


def pick_blocks(values, which, block_count):
    indicator_matrix = (which[:, None] == jnp.arange(block_count, dtype=jnp.int32)[None, :]).astype(
        jnp.float32
    )
    block_list = values.reshape(block_count, values.shape[0] // block_count, values.shape[1])
    return jnp.einsum("dq,qsp->dsp", indicator_matrix, block_list, precision=EXACT_PRECISION)


def insert_blocks(tile_collection, which, block_count):
    indicator_matrix = (which[:, None] == jnp.arange(block_count, dtype=jnp.int32)[None, :]).astype(
        jnp.float32
    )
    reduced_sum = jnp.einsum(
        "jx,jsv->xsv", indicator_matrix, tile_collection, precision=EXACT_PRECISION
    )
    return reduced_sum.reshape(block_count * tile_collection.shape[1], tile_collection.shape[2])


def item_terms(row_tiles, item_tiles, weight, offset, item_which, item_count):
    predicted = jnp.einsum("trk,tik->tri", row_tiles, item_tiles, precision=EXACT_PRECISION)
    leftover = weight * (1.0 - predicted)
    row_cols = lax.dynamic_slice_in_dim(row_tiles, offset, BLK, 2)
    tile_terms = jnp.einsum("tri,trj->tij", leftover, row_cols, precision=EXACT_PRECISION)
    return insert_blocks(tile_terms, item_which, item_count)


def item_product(row_cols, weight, direction, item_which, item_count):
    picked = pick_blocks(direction, item_which, item_count)
    inner_sum = jnp.einsum("trj,tij->tri", row_cols, picked, precision=EXACT_PRECISION)
    tile_terms = jnp.einsum("tri,trj->tij", weight * inner_sum, row_cols, precision=EXACT_PRECISION)
    return insert_blocks(tile_terms, item_which, item_count)


def row_terms(row_tiles, item_tiles, weight, offset, row_which, row_count):
    predicted = jnp.einsum("trk,tik->tri", row_tiles, item_tiles, precision=EXACT_PRECISION)
    leftover = weight * (1.0 - predicted)
    item_cols = lax.dynamic_slice_in_dim(item_tiles, offset, BLK, 2)
    tile_terms = jnp.einsum("tri,tij->trj", leftover, item_cols, precision=EXACT_PRECISION)
    return insert_blocks(tile_terms, row_which, row_count)


def row_product(item_cols, weight, direction, row_which, row_count):
    picked = pick_blocks(direction, row_which, row_count)
    inner_sum = jnp.einsum("trj,tij->tri", picked, item_cols, precision=EXACT_PRECISION)
    tile_terms = jnp.einsum(
        "tri,tij->trj", weight * inner_sum, item_cols, precision=EXACT_PRECISION
    )
    return insert_blocks(tile_terms, row_which, row_count)


def conjugate(right_side, operator_fn):
    result = jnp.zeros_like(right_side)
    leftover = right_side
    direction = right_side
    norm_now = jnp.sum(leftover * leftover, axis=1, keepdims=True)
    for iteration in range(CG_STEPS):
        applied = operator_fn(direction)
        step_length = norm_now / (jnp.sum(direction * applied, axis=1, keepdims=True) + EPSILON)
        result = result + step_length * direction
        leftover = leftover - step_length * applied
        norm_next = jnp.sum(leftover * leftover, axis=1, keepdims=True)
        direction = leftover + norm_next / (norm_now + EPSILON) * direction
        norm_now = norm_next
    return result


def local(
    user_emb,
    tag_emb,
    item_emb,
    user_tile_block,
    user_tile_item,
    user_tile_counts,
    tag_tile_block,
    tag_tile_item,
    tag_tile_counts,
):
    tile_size = user_tile_counts.shape[1]
    user_blocks = user_emb.shape[0] // tile_size
    tag_blocks = tag_emb.shape[0] // tile_size
    item_blocks = item_emb.shape[0] // tile_size
    user_total = user_emb.shape[0]
    offset = 0
    user_weight = CONFIDENCE * user_tile_counts.astype(jnp.float32)
    tag_weight = CONFIDENCE * tag_tile_counts.astype(jnp.float32)
    user_tiles = pick_blocks(user_emb, user_tile_block, user_blocks)
    tag_tiles = pick_blocks(tag_emb, tag_tile_block, tag_blocks)
    user_col_tiles = lax.dynamic_slice_in_dim(user_tiles, offset, BLK, 2)
    tag_col_tiles = lax.dynamic_slice_in_dim(tag_tiles, offset, BLK, 2)
    items_for_users = pick_blocks(item_emb, user_tile_item, item_blocks)
    items_for_tags = pick_blocks(item_emb, tag_tile_item, item_blocks)
    user_cols = lax.dynamic_slice_in_dim(user_emb, offset, BLK, 1)
    tag_cols = lax.dynamic_slice_in_dim(tag_emb, offset, BLK, 1)
    item_cols = lax.dynamic_slice_in_dim(item_emb, offset, BLK, 1)
    gram_part = jnp.einsum(
        "rj,rk->jk", user_cols, user_emb, precision=EXACT_PRECISION
    ) + jnp.einsum("rj,rk->jk", tag_cols, tag_emb, precision=EXACT_PRECISION)
    observed_part = item_terms(
        user_tiles, items_for_users, user_weight, offset, user_tile_item, item_blocks
    ) + item_terms(tag_tiles, items_for_tags, tag_weight, offset, tag_tile_item, item_blocks)
    gram_rows, observed = lax.psum((gram_part, observed_part), "ut")
    gram_square = lax.dynamic_slice_in_dim(gram_rows, offset, BLK, 1)
    item_right = (
        observed
        - UNSEEN_WEIGHT * jnp.einsum("ik,jk->ij", item_emb, gram_rows, precision=EXACT_PRECISION)
        - PENALTY * item_cols
    )

    def item_operator(direction):
        local_part = item_product(
            user_col_tiles, user_weight, direction, user_tile_item, item_blocks
        ) + item_product(tag_col_tiles, tag_weight, direction, tag_tile_item, item_blocks)
        return (
            lax.psum(local_part, "ut")
            + UNSEEN_WEIGHT
            * jnp.dot(
                direction,
                gram_square,
                precision=EXACT_PRECISION,
                preferred_element_type=jnp.float32,
            )
            + PENALTY * direction
        )

    item_block = item_cols + conjugate(item_right, item_operator)
    new_items = lax.dynamic_update_slice_in_dim(item_emb, item_block, offset, 1)
    new_for_users = pick_blocks(new_items, user_tile_item, item_blocks)
    new_for_tags = pick_blocks(new_items, tag_tile_item, item_blocks)
    user_item_cols = lax.dynamic_slice_in_dim(new_for_users, offset, BLK, 2)
    tag_item_cols = lax.dynamic_slice_in_dim(new_for_tags, offset, BLK, 2)
    gram_part_rows = jnp.einsum("ij,ik->jk", item_block, new_items, precision=EXACT_PRECISION)
    observed_rows = jnp.concatenate(
        [
            row_terms(user_tiles, new_for_users, user_weight, offset, user_tile_block, user_blocks),
            row_terms(tag_tiles, new_for_tags, tag_weight, offset, tag_tile_block, tag_blocks),
        ],
        axis=0,
    )
    all_rows = jnp.concatenate([user_emb, tag_emb], axis=0)
    row_cols = jnp.concatenate([user_cols, tag_cols], axis=0)

    def row_local(direction):
        return jnp.concatenate(
            [
                row_product(
                    user_item_cols,
                    user_weight,
                    direction[:user_total],
                    user_tile_block,
                    user_blocks,
                ),
                row_product(
                    tag_item_cols, tag_weight, direction[user_total:], tag_tile_block, tag_blocks
                ),
            ],
            axis=0,
        )

    item_gram, observed_sum = lax.psum((gram_part_rows, observed_rows), "it")
    item_square = lax.dynamic_slice_in_dim(item_gram, offset, BLK, 1)
    row_right = (
        observed_sum
        - UNSEEN_WEIGHT * jnp.einsum("rk,jk->rj", all_rows, item_gram, precision=EXACT_PRECISION)
        - PENALTY * row_cols
    )

    def row_operator(direction):
        return (
            lax.psum(row_local(direction), "it")
            + UNSEEN_WEIGHT
            * jnp.dot(
                direction,
                item_square,
                precision=EXACT_PRECISION,
                preferred_element_type=jnp.float32,
            )
            + PENALTY * direction
        )

    solution = row_cols + conjugate(row_right, row_operator)
    return (item_block, solution[:user_total], solution[user_total:])


BF16 = jnp.bfloat16
F32 = jnp.float32
MESH = pl.DeviceIdType.MESH


def halves(value):
    high = value.astype(BF16)
    return high, (value - high.astype(F32)).astype(BF16)


def dot_nt(left, right):
    return lax.dot_general(left, right, (((1,), (1,)), ((), ())), preferred_element_type=F32)


def dot_nn(left, right):
    return lax.dot_general(left, right, (((1,), (0,)), ((), ())), preferred_element_type=F32)


def stacked(value):
    return jnp.concatenate(halves(value), axis=0)


def paired(value):
    return jnp.concatenate(halves(value), axis=1)


def twice(value):
    both = stacked(value)
    return jnp.concatenate([both, both], axis=1)


def fold(total):
    rows = total.shape[0] // 2
    return total[:rows, :BLK] + total[:rows, BLK:] + total[rows:, :BLK] + total[rows:, BLK:]


def fold_rows(total):
    rows = total.shape[0] // 2
    return total[:rows] + total[rows:]


def solve(right_side, weight_ref, table_ref):
    chunks = weight_ref.shape[0]

    def step(_, carry):
        result, leftover, direction, norm_now = carry
        operand = twice(direction)
        total = None
        for j in range(chunks):
            inner = fold_rows(dot_nt(operand, table_ref[j]))
            term = dot_nn(stacked(weight_ref[j] * inner), table_ref[j])
            total = term if total is None else total + term
        applied = fold(total) + PENALTY * direction
        length = norm_now / (jnp.sum(direction * applied, axis=1, keepdims=True) + EPSILON)
        result = result + length * direction
        leftover = leftover - length * applied
        norm_next = jnp.sum(leftover * leftover, axis=1, keepdims=True)
        direction = leftover + norm_next / (norm_now + EPSILON) * direction
        return result, leftover, direction, norm_next

    norm = jnp.sum(right_side * right_side, axis=1, keepdims=True)
    start = (jnp.zeros_like(right_side), right_side, right_side, norm)
    return lax.fori_loop(0, CG_STEPS, step, start)[0]


def kernel(
    nu, ni, total_copies,
    ub_ref, ui_ref, tb_ref, ti_ref,
    user_ref, tag_ref, item_ref, uc_ref, tc_ref,
    item_out, user_out, tag_out,
    place, place_u, place_i, at, rat, ar, rar, wj, w2, hh, hl, e0, re0, est, part, rpart,
    at_own, a_own, ib, ib2, out, send_sem, recv_sem,
):
    k = lax.axis_index("ut")
    m = lax.axis_index("it")
    tile = uc_ref.shape[1]
    ut, tt = uc_ref.shape[0], tc_ref.shape[0]
    users, tags, items = user_ref.shape[0], tag_ref.shape[0], item_ref.shape[0]
    nub, ntb, nib = users // tile, tags // tile, items // tile
    nrb = nub + ntb
    rows = users + tags
    sub_i, sub_r = tile // nu, tile // ni
    share = rows // ni
    chips = ni // 2
    chip, core = m // 2, m % 2
    other = 1 - core
    sibling = 2 * chip + other

    def u_to(d):
        return (k + d) % nu

    def u_from(d):
        return (k + nu - d) % nu

    def i_to(d):
        return (m + d) % ni

    def i_from(d):
        return (m + ni - d) % ni

    def c_to(d):
        return (chip + d) % chips

    def c_from(d):
        return (chip + chips - d) % chips

    sent = []
    count = [0]

    def ticket():
        count[0] += 1
        return count[0] - 1

    def copy(number, source, target, device):
        return pltpu.make_async_remote_copy(
            src_ref=source, dst_ref=target, send_sem=send_sem.at[number],
            recv_sem=recv_sem.at[number], device_id=device, device_id_type=MESH,
        )

    def send(number, source, target, device):
        moving = copy(number, source, target, device)
        moving.start()
        sent.append(moving)

    def arrived(number, target):
        copy(number, target, target, (u_to(1), m)).wait_recv()

    barrier = pltpu.get_barrier_semaphore()
    for d in range(1, nu):
        pl.semaphore_signal(barrier, inc=1, device_id=(u_to(d), m), device_id_type=MESH)
    for d in range(1, ni):
        pl.semaphore_signal(barrier, inc=1, device_id=(k, i_to(d)), device_id_type=MESH)

    wj[k, 0:users, :] = user_ref[:, 0:BLK]
    wj[k, users:rows, :] = tag_ref[:, 0:BLK]
    line = lax.broadcasted_iota(jnp.int32, place.shape, 0)
    spots = jnp.zeros(place.shape, jnp.int32)
    for t in range(ut):
        spots = jnp.where(line == t, ub_ref[t] * nib + ui_ref[t], spots)
    for t in range(tt):
        spots = jnp.where(line == ut + t, (nub + tb_ref[t]) * nib + ti_ref[t], spots)
    place[...] = spots
    for t in range(ut + tt):
        counts = CONFIDENCE * (uc_ref[t] if t < ut else tc_ref[t - ut]).astype(F32)
        ar[t] = counts
        at[t] = counts.T

    pl.semaphore_wait(barrier, nu + ni - 2)

    def w_slice(kk, mm):
        return wj.at[kk, pl.ds(pl.multiple_of(mm * share, 8), share), :]

    def b_slice(kk, mm):
        return ib.at[mm, :, pl.ds(pl.multiple_of(kk * sub_i, 8), sub_i), :]

    far = sorted(range(1, nu), key=lambda d: min(d, nu - d))

    def tickets(first):
        z = {d: ticket() for d in range(1, nu)}
        p = {(d, e): ticket() for d in range(first, nu) for e in range(1, chips)}
        s = {(d, e): ticket() for d in range(first, nu) for e in range(chips)}
        return z, p, s

    def spread_along(piece, marks):
        for d in far:
            send(marks[0][d], piece(k, m), piece(k, m), (u_to(d), m))

    def spread_plane(piece, marks, d):
        held = piece(u_from(d), m)
        for e in range(1, chips):
            send(marks[1][d, e], held, held, (k, 2 * c_to(e) + core))
        send(marks[2][d, 0], held, held, (k, sibling))

    def spread_sibling(piece, marks, d):
        for e in range(1, chips):
            held = piece(u_from(d), 2 * c_from(e) + core)
            arrived(marks[1][d, e], held)
            send(marks[2][d, e], held, held, (k, sibling))

    def spread_finish(piece, marks, d):
        for e in range(chips):
            arrived(marks[2][d, e], piece(u_from(d), 2 * c_from(e) + other))

    w_marks = tickets(1)
    spread_along(w_slice, w_marks)
    at_marks = {d: (ticket(), ticket()) for d in range(1, nu)}

    def at_cut(kk):
        return at.at[:, pl.ds(pl.multiple_of(kk * sub_i, 8), sub_i), :]

    def r_cut(ref, mm):
        return ref.at[:, pl.ds(pl.multiple_of(mm * sub_r, 8), sub_r), :]

    for d in far:
        send(at_marks[d][0], at_cut(u_to(d)), rat.at[k], (u_to(d), m))
        send(at_marks[d][1], place, place_u.at[k], (u_to(d), m))
    ar_marks = {d: (ticket(), ticket()) for d in range(1, ni)}
    for d in range(1, ni):
        send(ar_marks[d][0], r_cut(ar, i_to(d)), rar.at[m], (k, i_to(d)))
        send(ar_marks[d][1], place, place_i.at[m], (k, i_to(d)))
    rat[k] = at[:, pl.ds(pl.multiple_of(k * sub_i, 8), sub_i), :]
    rar[m] = ar[:, pl.ds(pl.multiple_of(m * sub_r, 8), sub_r), :]
    place_u[k] = place[...]
    place_i[m] = place[...]

    def dense(spot_rows, tiles, block, piece):
        total = None
        for t in (range(ut) if block < nub else range(ut, ut + tt)):
            code = block * nib + piece
            term = jnp.where(spot_rows[t : t + 1, :] == code, tiles(t), 0.0)
            total = term if total is None else total + term
        return total

    high, low = halves(item_ref[...])
    hh[...] = high
    hl[...] = low
    spot_rows = place[...]
    step = 2 if nub % 2 == 0 and ntb % 2 == 0 else 1

    def terms(first):
        block = user_ref[first * tile : (first + step) * tile, :] if first < nub else (
            tag_ref[(first - nub) * tile : (first - nub + step) * tile, :])
        rh, rl = halves(block)

        def product(cols):
            return (dot_nt(rh[:, cols], hh[:, cols]) + dot_nt(rh[:, cols], hl[:, cols])
                    + dot_nt(rl[:, cols], hh[:, cols]))

        rest = product(slice(BLK, None))
        mine = product(slice(0, BLK))
        counts = jnp.concatenate([
            jnp.concatenate([dense(spot_rows, lambda t: ar[t], b, p) for p in range(nib)], axis=1)
            for b in range(first, first + step)], axis=0)
        weight = counts + UNSEEN_WEIGHT
        begun = counts - weight * rest
        leftover = (begun - weight * mine).T
        eh, el = halves(leftover)
        span = slice(first * tile, (first + step) * tile)
        est[0:items, span] = eh
        est[items:, span] = el
        for b in range(step):
            e0[first + b] = begun[b * tile : (b + 1) * tile]

    firsts = list(range(0, nrb, step))
    for first in firsts[: len(firsts) // 2]:
        terms(first)
    for d in far:
        arrived(w_marks[0][d], w_slice(u_from(d), m))
        spread_plane(w_slice, w_marks, d)
    for first in firsts[len(firsts) // 2 :]:
        terms(first)
    w2[k] = paired(wj[k])
    summed = fold(dot_nn(est[...], w2[k]))
    for p in range(nib):
        part[p] = summed[p * tile : (p + 1) * tile]
    p_marks = {d: ticket() for d in range(1, nu)}
    for d in far:
        send(p_marks[d], at_like(part, u_to(d), sub_i), rpart.at[k], (u_to(d), m))
    rpart[k] = part[:, pl.ds(pl.multiple_of(k * sub_i, 8), sub_i), :]
    for d in far:
        spread_sibling(w_slice, w_marks, d)
    e_marks = {d: ticket() for d in range(1, ni)}
    for d in range(1, ni):
        send(e_marks[d], r_cut(e0, i_to(d)), re0.at[m], (k, i_to(d)))
    re0[m] = e0[:, pl.ds(pl.multiple_of(m * sub_r, 8), sub_r), :]

    for d in far:
        arrived(at_marks[d][0], rat.at[u_from(d)])
        arrived(at_marks[d][1], place_u.at[u_from(d)])

    def lay_items(kk, none):
        spot = place_u[kk]
        for p in range(nib):
            for b in range(nrb):
                at_own[kk, p * sub_i : (p + 1) * sub_i, b * tile : (b + 1) * tile] = (
                    dense(spot, lambda t: rat[kk, t], b, p) + UNSEEN_WEIGHT)
        return none

    lax.fori_loop(0, nu, lay_items, 0)
    for d in far:
        spread_finish(w_slice, w_marks, d)
        source = u_from(d)
        w2[source] = paired(wj[source])
    for d in far:
        arrived(p_marks[d], rpart.at[u_from(d)])
    observed = rpart[0]
    for kk in range(1, nu):
        observed = observed + rpart[kk]
    own_items = jnp.concatenate([
        item_ref[pl.ds(pl.multiple_of(p * tile + k * sub_i, 8), sub_i), 0:BLK] for p in range(nib)], axis=0)
    right = observed.reshape(nib * sub_i, BLK) - PENALTY * own_items
    block = own_items + solve(right, at_own, w2)
    ib[m, :, pl.ds(pl.multiple_of(k * sub_i, 8), sub_i), :] = block.reshape(nib, sub_i, BLK)

    b_marks = tickets(0)
    spread_along(b_slice, b_marks)
    spread_plane(b_slice, b_marks, 0)
    for d in range(1, ni):
        arrived(ar_marks[d][0], rar.at[i_from(d)])
        arrived(ar_marks[d][1], place_i.at[i_from(d)])

    for d in far:
        arrived(b_marks[0][d], b_slice(u_from(d), m))
        spread_plane(b_slice, b_marks, d)

    def lay_rows(mm, none):
        spot = place_i[mm]
        for b in range(nrb):
            for p in range(nib):
                a_own[mm, b * sub_r : (b + 1) * sub_r, p * tile : (p + 1) * tile] = (
                    dense(spot, lambda t: rar[mm, t], b, p) + UNSEEN_WEIGHT)
        return none

    lax.fori_loop(0, ni, lay_rows, 0)
    for d in [0] + far:
        spread_sibling(b_slice, b_marks, d)
    for d in range(1, ni):
        arrived(e_marks[d], re0.at[i_from(d)])
    own_rows = jnp.concatenate(
        [user_ref[pl.ds(pl.multiple_of(b * tile + m * sub_r, 8), sub_r), 0:BLK] for b in range(nub)]
        + [tag_ref[pl.ds(pl.multiple_of(b * tile + m * sub_r, 8), sub_r), 0:BLK] for b in range(ntb)], axis=0)
    operand = twice(own_rows)
    for d in [0] + far:
        spread_finish(b_slice, b_marks, d)

    def gather(mm, total):
        table = paired(ib[mm].reshape(items, BLK))
        ib2[mm] = table
        inner = fold_rows(dot_nt(operand, table))
        leftover = re0[mm].reshape(share, items) - a_own[mm] * inner
        return total + dot_nn(stacked(leftover), table)

    total = lax.fori_loop(0, ni, gather, jnp.zeros((2 * share, 2 * BLK), F32))
    right = fold(total) - PENALTY * own_rows
    final = own_rows + solve(right, a_own, ib2)
    out[:, pl.ds(pl.multiple_of(m * sub_r, 8), sub_r), :] = final.reshape(nrb, sub_r, BLK)
    o_marks = {d: ticket() for d in range(1, ni)}
    for d in range(1, ni):
        send(o_marks[d], r_cut(out, m), r_cut(out, m), (k, i_to(d)))
    item_out[...] = ib[m].reshape(items, BLK)
    for d in range(1, ni):
        arrived(o_marks[d], r_cut(out, i_from(d)))
    for b in range(nub):
        user_out[b * tile : (b + 1) * tile, :] = out[b]
    for b in range(ntb):
        tag_out[b * tile : (b + 1) * tile, :] = out[nub + b]
    for moving in sent:
        moving.wait_send()
    if count[0] != total_copies:
        raise ValueError(count[0])


def at_like(ref, index, size):
    return ref.at[:, pl.ds(pl.multiple_of(index * size, 8), size), :]


def fused(
    nu, ni, user_emb, tag_emb, item_emb, user_tile_block, user_tile_item, user_tile_counts,
    tag_tile_block, tag_tile_item, tag_tile_counts,
):
    tile = user_tile_counts.shape[1]
    tiles = user_tile_counts.shape[0] + tag_tile_counts.shape[0]
    users, tags, (items, rank) = user_emb.shape[0], tag_emb.shape[0], item_emb.shape
    rows = users + tags
    nrb, nib = rows // tile, items // tile
    sub_i, sub_r, share, chips = tile // nu, tile // ni, rows // ni, ni // 2
    lines = -(-tiles // 8) * 8
    copies = (
        (nu - 1) + (nu - 1) * (2 * chips - 1) + (nu - 1) + nu * (2 * chips - 1)
        + 3 * (nu - 1) + 4 * (ni - 1)
    )
    vmem = pl.BlockSpec(memory_space=pltpu.VMEM)
    smem = pl.BlockSpec(memory_space=pltpu.SMEM)
    return pl.pallas_call(
        functools.partial(kernel, nu, ni, copies),
        out_shape=(
            jax.ShapeDtypeStruct((items, BLK), F32),
            jax.ShapeDtypeStruct((users, BLK), F32),
            jax.ShapeDtypeStruct((tags, BLK), F32),
        ),
        in_specs=[smem] * 4 + [vmem] * 5,
        out_specs=(vmem, vmem, vmem),
        scratch_shapes=[
            pltpu.VMEM((lines, 128), jnp.int32),
            pltpu.VMEM((nu, lines, 128), jnp.int32),
            pltpu.VMEM((ni, lines, 128), jnp.int32),
            pltpu.VMEM((tiles, tile, tile), F32),
            pltpu.VMEM((nu, tiles, sub_i, tile), F32),
            pltpu.VMEM((tiles, tile, tile), F32),
            pltpu.VMEM((ni, tiles, sub_r, tile), F32),
            pltpu.VMEM((nu, rows, BLK), F32),
            pltpu.VMEM((nu, rows, 2 * BLK), BF16),
            pltpu.VMEM((items, rank), BF16),
            pltpu.VMEM((items, rank), BF16),
            pltpu.VMEM((nrb, tile, items), F32),
            pltpu.VMEM((ni, nrb, sub_r, items), F32),
            pltpu.VMEM((2 * items, rows), BF16),
            pltpu.VMEM((nib, tile, BLK), F32),
            pltpu.VMEM((nu, nib, sub_i, BLK), F32),
            pltpu.VMEM((nu, nib * sub_i, rows), F32),
            pltpu.VMEM((ni, share, items), F32),
            pltpu.VMEM((ni, nib, tile, BLK), F32),
            pltpu.VMEM((ni, items, 2 * BLK), BF16),
            pltpu.VMEM((nrb, tile, BLK), F32),
            pltpu.SemaphoreType.DMA((copies,)),
            pltpu.SemaphoreType.DMA((copies,)),
        ],
        compiler_params=pltpu.CompilerParams(
            collective_id=0, has_side_effects=True, vmem_limit_bytes=48 * 1024 * 1024
        ),
    )(
        user_tile_block, user_tile_item, tag_tile_block, tag_tile_item,
        user_emb, tag_emb, item_emb, user_tile_counts, tag_tile_counts,
    )


def serves(nu, ni, tile):
    return nu > 1 and ni > 2 and ni % 2 == 0 and tile % (nu * 8) == 0 and tile % (ni * 16) == 0


def solution(mesh):
    placed = (
        P("ut", None),
        P("ut", None),
        P("it", None),
        P(("ut", "it")),
        P(("ut", "it")),
        P(("ut", "it"), None, None),
        P(("ut", "it")),
        P(("ut", "it")),
        P(("ut", "it"), None, None),
    )
    nu, ni = mesh.shape["ut"], mesh.shape["it"]

    def run(*arrays):
        if serves(nu, ni, arrays[5].shape[1]):
            return fused(nu, ni, *arrays)
        return local(*arrays)

    return jax.shard_map(
        run,
        mesh=mesh,
        in_specs=placed,
        out_specs=(P("it", None), P("ut", None), P("ut", None)),
        check_vma=False,
    )
```

profile of v0, /device:TPU:1, one launch (start us, length us, event | category | flops | bytes accessed | tf_op | source)
XLA Modules:
  0.0 60.7 jit_solution(15186547220345749447)
XLA Ops:
  0.6 0.0 copy-start
  0.6 1.2 %copy-done = f32[512,512]{1,0:T(8,128)S(1)} copy-done((f32[512,512]{1,0:T(8,128)S(1)}, f32[512,512]{1,0:T(8,128)}, u32[]{:S(2)}) %copy-start) | copy-done | bytes 1048600
  1.9 0.0 copy-start.1
  1.9 1.0 %copy-done.1 = f32[256,512]{1,0:T(8,128)S(1)} copy-done((f32[256,512]{1,0:T(8,128)S(1)}, f32[256,512]{1,0:T(8,128)}, u32[]{:S(2)}) %copy-start.1) | copy-done | bytes 524312
  2.9 0.0 copy-start.2
  2.9 1.0 %copy-done.2 = f32[256,512]{1,0:T(8,128)S(1)} copy-done((f32[256,512]{1,0:T(8,128)S(1)}, f32[256,512]{1,0:T(8,128)}, u32[]{:S(2)}) %copy-start.2) | copy-done | bytes 524312
  3.9 0.0 copy-start.3
  3.9 0.9 %copy-done.3 = s32[4,128,128]{2,1,0:T(8,128)S(1)} copy-done((s32[4,128,128]{2,1,0:T(8,128)S(1)}, s32[4,128,128]{2,1,0:T(8,128)}, u32[]{:S(2)}) %copy-start.3) | copy-done | bytes 262168
  4.9 0.0 copy-start.4
  4.9 0.9 %copy-done.4 = s32[2,128,128]{2,1,0:T(8,128)S(1)} copy-done((s32[2,128,128]{2,1,0:T(8,128)S(1)}, s32[2,128,128]{2,1,0:T(8,128)}, u32[]{:S(2)}) %copy-start.4) | copy-done | bytes 131096
  5.8 0.0 copy-start.5
  5.8 0.7 %copy-done.5 = s32[4]{0:T(128)S(1)} copy-done((s32[4]{0:T(128)S(1)}, s32[4]{0:T(128)}, u32[]{:S(2)}) %copy-start.5) | copy-done | bytes 40
  6.5 0.0 copy-start.6
  6.5 0.7 %copy-done.6 = s32[4]{0:T(128)S(1)} copy-done((s32[4]{0:T(128)S(1)}, s32[4]{0:T(128)}, u32[]{:S(2)}) %copy-start.6) | copy-done | bytes 40
  7.1 0.0 copy-start.7
  7.1 0.7 %copy-done.7 = s32[2]{0:T(128)S(1)} copy-done((s32[2]{0:T(128)S(1)}, s32[2]{0:T(128)}, u32[]{:S(2)}) %copy-start.7) | copy-done | bytes 32
  7.8 0.0 copy-start.8
  7.8 0.7 %copy-done.8 = s32[2]{0:T(128)S(1)} copy-done((s32[2]{0:T(128)S(1)}, s32[2]{0:T(128)}, u32[]{:S(2)}) %copy-start.8) | copy-done | bytes 32
  8.4 50.3 %shard_map.112 = (f32[256,128]{1,0:T(8,128)S(1)}, f32[512,128]{1,0:T(8,128)S(1)}, f32[256,128]{1,0:T(8,128)S(1)}) custom-call(s32[4]{0:T(128)S(1)} %copy-done.5, s32[4]{0:T(128)S(1)} %copy-done.6, s32[2]{0:T(128)S(1)} %copy-done.7, s32[2]{0:T(128)S(1)} %copy-done.8, f32[512,512]{1,0:T(8,128)S(1)} %copy-done, f32[256,512]{1,0:T(8,128)S(1)} %copy-done.1, ...), custom_call_target="tpu_custom_call" | custom-call | tf_op jit(solution)/shard_map/pallas_call | solution.py:577
  58.7 0.7 %copy.15 = f32[256,128]{1,0:T(8,128)} copy(f32[256,128]{1,0:T(8,128)S(1)} %get-tuple-element.6) | data formatting | bytes 262144
  59.4 0.7 %copy.16 = f32[512,128]{1,0:T(8,128)} copy(f32[512,128]{1,0:T(8,128)S(1)} %get-tuple-element.7) | data formatting | bytes 524288
  60.1 0.7 %copy.17 = f32[256,128]{1,0:T(8,128)} copy(f32[256,128]{1,0:T(8,128)S(1)} %get-tuple-element.8) | data formatting | bytes 262144
Async XLA Ops:
  0.6 1.2 %copy-start = (f32[512,512]{1,0:T(8,128)S(1)}, f32[512,512]{1,0:T(8,128)}, u32[]{:S(2)}) copy-start(f32[512,512]{1,0:T(8,128)} %user_ref.1) | copy-start | bytes 3145732
  1.9 1.0 %copy-start.1 = (f32[256,512]{1,0:T(8,128)S(1)}, f32[256,512]{1,0:T(8,128)}, u32[]{:S(2)}) copy-start(f32[256,512]{1,0:T(8,128)} %tag_ref.1) | copy-start | bytes 1572868
  2.9 1.0 %copy-start.2 = (f32[256,512]{1,0:T(8,128)S(1)}, f32[256,512]{1,0:T(8,128)}, u32[]{:S(2)}) copy-start(f32[256,512]{1,0:T(8,128)} %item_ref.1) | copy-start | bytes 1572868
  3.9 0.9 %copy-start.3 = (s32[4,128,128]{2,1,0:T(8,128)S(1)}, s32[4,128,128]{2,1,0:T(8,128)}, u32[]{:S(2)}) copy-start(s32[4,128,128]{2,1,0:T(8,128)} %uc_ref.1) | copy-start | bytes 786436
  4.9 0.9 %copy-start.4 = (s32[2,128,128]{2,1,0:T(8,128)S(1)}, s32[2,128,128]{2,1,0:T(8,128)}, u32[]{:S(2)}) copy-start(s32[2,128,128]{2,1,0:T(8,128)} %tc_ref.1) | copy-start | bytes 393220
  5.8 0.7 %copy-start.5 = (s32[4]{0:T(128)S(1)}, s32[4]{0:T(128)}, u32[]{:S(2)}) copy-start(s32[4]{0:T(128)} %ub_ref.1) | copy-start | bytes 52
  6.5 0.7 %copy-start.6 = (s32[4]{0:T(128)S(1)}, s32[4]{0:T(128)}, u32[]{:S(2)}) copy-start(s32[4]{0:T(128)} %ui_ref.1) | copy-start | bytes 52
  7.1 0.7 %copy-start.7 = (s32[2]{0:T(128)S(1)}, s32[2]{0:T(128)}, u32[]{:S(2)}) copy-start(s32[2]{0:T(128)} %tb_ref.1) | copy-start | bytes 28
  7.8 0.7 %copy-start.8 = (s32[2]{0:T(128)S(1)}, s32[2]{0:T(128)}, u32[]{:S(2)}) copy-start(s32[2]{0:T(128)} %ti_ref.1) | copy-start | bytes 28
where the time goes:
time: 61.1 us; the launch traced here: 60.7 us
  Pallas kernels  50.3 us (82%)
  local copies, waits for them, and re-layouts  9.79 us (16%)
  between operations  0.66 us (1%)
    pallas_call x1, Pallas kernels, fused(): pl.pallas_call(functools.partial(kernel, nu, ni, copies), out_shape=(jax....  50.3 us
    unnamed x21, local copies, waits for them, and re-layouts  9.79 us

commit v1 on v0

--- a/solution.py
+++ b/solution.py
@@ -268,9 +268,10 @@
 
 def kernel(
     nu, ni, total_copies,
-    ub_ref, ui_ref, tb_ref, ti_ref,
-    user_ref, tag_ref, item_ref, uc_ref, tc_ref,
+    ub_hbm, ui_hbm, tb_hbm, ti_hbm,
+    user_hbm, tag_hbm, item_hbm, uc_hbm, tc_hbm,
     item_out, user_out, tag_out,
+    ub_ref, ui_ref, tb_ref, ti_ref, user_ref, tag_ref, item_ref, uc_ref, tc_ref, local_sem,
     place, place_u, place_i, at, rat, ar, rar, wj, w2, hh, hl, e0, re0, est, part, rpart,
     at_own, a_own, ib, ib2, out, send_sem, recv_sem,
 ):
@@ -334,8 +335,16 @@
     for d in range(1, ni):
         pl.semaphore_signal(barrier, inc=1, device_id=(k, i_to(d)), device_id_type=MESH)
 
-    wj[k, 0:users, :] = user_ref[:, 0:BLK]
-    wj[k, users:rows, :] = tag_ref[:, 0:BLK]
+    pairs = (
+        (user_hbm.at[:, 0:BLK], wj.at[k, 0:users, :]), (tag_hbm.at[:, 0:BLK], wj.at[k, users:rows, :]),
+        (ub_hbm, ub_ref), (ui_hbm, ui_ref), (tb_hbm, tb_ref), (ti_hbm, ti_ref),
+        (uc_hbm, uc_ref), (tc_hbm, tc_ref), (item_hbm, item_ref), (user_hbm, user_ref), (tag_hbm, tag_ref),
+    )
+    loads = [pltpu.make_async_copy(a, b, local_sem.at[i]) for i, (a, b) in enumerate(pairs)]
+    for load in loads:
+        load.start()
+    for load in loads[2:8]:
+        load.wait()
     line = lax.broadcasted_iota(jnp.int32, place.shape, 0)
     spots = jnp.zeros(place.shape, jnp.int32)
     for t in range(ut):
@@ -348,6 +357,8 @@
         ar[t] = counts
         at[t] = counts.T
 
+    for load in loads[:2]:
+        load.wait()
     pl.semaphore_wait(barrier, nu + ni - 2)
 
     def w_slice(kk, mm):
@@ -414,6 +425,8 @@
             total = term if total is None else total + term
         return total
 
+    for load in loads[8:]:
+        load.wait()
     high, low = halves(item_ref[...])
     hh[...] = high
     hl[...] = low
@@ -480,6 +493,19 @@
         return none
 
     lax.fori_loop(0, nu, lay_items, 0)
+    for d in range(1, ni):
+        arrived(ar_marks[d][0], rar.at[i_from(d)])
+        arrived(ar_marks[d][1], place_i.at[i_from(d)])
+
+    def lay_rows(mm, none):
+        spot = place_i[mm]
+        for b in range(nrb):
+            for p in range(nib):
+                a_own[mm, b * sub_r : (b + 1) * sub_r, p * tile : (p + 1) * tile] = (
+                    dense(spot, lambda t: rar[mm, t], b, p) + UNSEEN_WEIGHT)
+        return none
+
+    lax.fori_loop(0, ni, lay_rows, 0)
     for d in far:
         spread_finish(w_slice, w_marks, d)
         source = u_from(d)
@@ -495,58 +521,66 @@
     block = own_items + solve(right, at_own, w2)
     ib[m, :, pl.ds(pl.multiple_of(k * sub_i, 8), sub_i), :] = block.reshape(nib, sub_i, BLK)
 
-    b_marks = tickets(0)
-    spread_along(b_slice, b_marks)
-    spread_plane(b_slice, b_marks, 0)
-    for d in range(1, ni):
-        arrived(ar_marks[d][0], rar.at[i_from(d)])
-        arrived(ar_marks[d][1], place_i.at[i_from(d)])
-
-    for d in far:
-        arrived(b_marks[0][d], b_slice(u_from(d), m))
-        spread_plane(b_slice, b_marks, d)
-
-    def lay_rows(mm, none):
-        spot = place_i[mm]
-        for b in range(nrb):
-            for p in range(nib):
-                a_own[mm, b * sub_r : (b + 1) * sub_r, p * tile : (p + 1) * tile] = (
-                    dense(spot, lambda t: rar[mm, t], b, p) + UNSEEN_WEIGHT)
-        return none
-
-    lax.fori_loop(0, ni, lay_rows, 0)
-    for d in [0] + far:
-        spread_sibling(b_slice, b_marks, d)
-    for d in range(1, ni):
-        arrived(e_marks[d], re0.at[i_from(d)])
     own_rows = jnp.concatenate(
         [user_ref[pl.ds(pl.multiple_of(b * tile + m * sub_r, 8), sub_r), 0:BLK] for b in range(nub)]
         + [tag_ref[pl.ds(pl.multiple_of(b * tile + m * sub_r, 8), sub_r), 0:BLK] for b in range(ntb)], axis=0)
     operand = twice(own_rows)
-    for d in [0] + far:
-        spread_finish(b_slice, b_marks, d)
+
+    b_marks = tickets(0)
+    spread_along(b_slice, b_marks)
+    spread_plane(b_slice, b_marks, 0)
+    for d in far:
+        arrived(b_marks[0][d], b_slice(u_from(d), m))
+        spread_plane(b_slice, b_marks, d)
+    for d in range(1, ni):
+        arrived(e_marks[d], re0.at[i_from(d)])
 
     def gather(mm, total):
         table = paired(ib[mm].reshape(items, BLK))
         ib2[mm] = table
         inner = fold_rows(dot_nt(operand, table))
         leftover = re0[mm].reshape(share, items) - a_own[mm] * inner
-        return total + dot_nn(stacked(leftover), table)
-
-    total = lax.fori_loop(0, ni, gather, jnp.zeros((2 * share, 2 * BLK), F32))
+        term = dot_nn(stacked(leftover), table)
+        return term if total is None else total + term
+
+    spread_sibling(b_slice, b_marks, 0)
+    total = gather(m, None)
+    for d in far:
+        spread_sibling(b_slice, b_marks, d)
+    for e in range(1, chips):
+        total = gather(2 * c_from(e) + core, total)
+    for e in range(chips):
+        for d in [0] + far:
+            arrived(b_marks[2][d, e], b_slice(u_from(d), 2 * c_from(e) + other))
+        total = gather(2 * c_from(e) + other, total)
     right = fold(total) - PENALTY * own_rows
     final = own_rows + solve(right, a_own, ib2)
     out[:, pl.ds(pl.multiple_of(m * sub_r, 8), sub_r), :] = final.reshape(nrb, sub_r, BLK)
-    o_marks = {d: ticket() for d in range(1, ni)}
-    for d in range(1, ni):
-        send(o_marks[d], r_cut(out, m), r_cut(out, m), (k, i_to(d)))
-    item_out[...] = ib[m].reshape(items, BLK)
-    for d in range(1, ni):
-        arrived(o_marks[d], r_cut(out, i_from(d)))
+    mine = r_cut(out, m)
+    o_marks = {e: ticket() for e in range(1, chips)}
+    x_marks = {e: ticket() for e in range(chips)}
+    for e in range(1, chips):
+        send(o_marks[e], mine, mine, (k, 2 * c_to(e) + core))
+    send(x_marks[0], mine, mine, (k, sibling))
+
+    def leave(i, source, target):
+        moving = pltpu.make_async_copy(source, target, local_sem.at[i])
+        moving.start()
+        return moving
+
+    leaving = [leave(p, ib.at[m, p], item_out.at[p * tile : (p + 1) * tile, :]) for p in range(nib)]
+    for e in range(1, chips):
+        held = r_cut(out, 2 * c_from(e) + core)
+        arrived(o_marks[e], held)
+        send(x_marks[e], held, held, (k, sibling))
+    for e in range(chips):
+        arrived(x_marks[e], r_cut(out, 2 * c_from(e) + other))
     for b in range(nub):
-        user_out[b * tile : (b + 1) * tile, :] = out[b]
+        leaving.append(leave(nib + b, out.at[b], user_out.at[b * tile : (b + 1) * tile, :]))
     for b in range(ntb):
-        tag_out[b * tile : (b + 1) * tile, :] = out[nub + b]
+        leaving.append(leave(nib + nub + b, out.at[nub + b], tag_out.at[b * tile : (b + 1) * tile, :]))
+    for moving in leaving:
+        moving.wait()
     for moving in sent:
         moving.wait_send()
     if count[0] != total_copies:
@@ -570,10 +604,9 @@
     lines = -(-tiles // 8) * 8
     copies = (
         (nu - 1) + (nu - 1) * (2 * chips - 1) + (nu - 1) + nu * (2 * chips - 1)
-        + 3 * (nu - 1) + 4 * (ni - 1)
-    )
-    vmem = pl.BlockSpec(memory_space=pltpu.VMEM)
-    smem = pl.BlockSpec(memory_space=pltpu.SMEM)
+        + 3 * (nu - 1) + 3 * (ni - 1) + 2 * chips - 1
+    )
+    hbm = pl.BlockSpec(memory_space=pltpu.HBM)
     return pl.pallas_call(
         functools.partial(kernel, nu, ni, copies),
         out_shape=(
@@ -581,9 +614,19 @@
             jax.ShapeDtypeStruct((users, BLK), F32),
             jax.ShapeDtypeStruct((tags, BLK), F32),
         ),
-        in_specs=[smem] * 4 + [vmem] * 5,
-        out_specs=(vmem, vmem, vmem),
+        in_specs=[hbm] * 9,
+        out_specs=(hbm, hbm, hbm),
         scratch_shapes=[
+            pltpu.SMEM(user_tile_block.shape, jnp.int32),
+            pltpu.SMEM(user_tile_item.shape, jnp.int32),
+            pltpu.SMEM(tag_tile_block.shape, jnp.int32),
+            pltpu.SMEM(tag_tile_item.shape, jnp.int32),
+            pltpu.VMEM(user_emb.shape, F32),
+            pltpu.VMEM(tag_emb.shape, F32),
+            pltpu.VMEM(item_emb.shape, F32),
+            pltpu.VMEM(user_tile_counts.shape, jnp.int32),
+            pltpu.VMEM(tag_tile_counts.shape, jnp.int32),
+            pltpu.SemaphoreType.DMA((max(11, nib + nrb),)),
             pltpu.VMEM((lines, 128), jnp.int32),
             pltpu.VMEM((nu, lines, 128), jnp.int32),
             pltpu.VMEM((ni, lines, 128), jnp.int32),
@@ -609,7 +652,7 @@
             pltpu.SemaphoreType.DMA((copies,)),
         ],
         compiler_params=pltpu.CompilerParams(
-            collective_id=0, has_side_effects=True, vmem_limit_bytes=48 * 1024 * 1024
+            collective_id=0, has_side_effects=True, vmem_limit_bytes=64 * 1024 * 1024
         ),
     )(
         user_tile_block, user_tile_item, tag_tile_block, tag_tile_item,

time: 61.1 us -> 51.9 us (0.85)
  local copies, waits for them, and re-layouts: 9.79 us -> 3.27 us
  Pallas kernels: 50.3 us -> 47.8 us
    unnamed x21 -> x7, local copies, waits for them, and re-layouts: 9.79 us -> 3.27 us
    pallas_call x1, Pallas kernels: 50.3 us -> 47.8 us  [fused(): pl.pallas_call(functools.partial(kernel, nu, ni, copies), out_shape=(jax....]
where the time goes in v1:
time: 51.9 us; the launch traced here: 51.7 us
  Pallas kernels  47.8 us (92%)
  local copies, waits for them, and re-layouts  3.27 us (6%)
  between operations  0.65 us (1%)
    pallas_call x1, Pallas kernels, fused(): pl.pallas_call(functools.partial(kernel, nu, ni, copies), out_shape=(jax....  47.8 us
    unnamed x7, local copies, waits for them, and re-layouts  3.27 us

profile of v1, /device:TPU:1, one launch (start us, length us, event | category | flops | bytes accessed | tf_op | source)
XLA Modules:
  0.0 51.7 jit_solution(8915465501769015685)
XLA Ops:
  0.6 47.8 %shard_map.112 = (f32[256,128]{1,0:T(8,128)}, f32[512,128]{1,0:T(8,128)}, f32[256,128]{1,0:T(8,128)}) custom-call(s32[4]{0:T(128)} %ub_hbm.1, s32[4]{0:T(128)} %ui_hbm.1, s32[2]{0:T(128)} %tb_hbm.1, s32[2]{0:T(128)} %ti_hbm.1, f32[512,512]{1,0:T(8,128)} %user_hbm.1, f32[256,512]{1,0:T(8,128)} %tag_hbm.1, f32[256,512]{1,0:T(8,128)} %item_hbm.1, ...), custom_call_target="tpu_custom_call" | custom-call | tf_op jit(solution)/shard_map/pallas_call | solution.py:610
  48.4 0.0 copy-start
  48.5 1.6 %copy.15 = f32[256,128]{1,0:T(8,128)} copy(f32[256,128]{1,0:T(8,128)} %get-tuple-element.6) | data formatting | bytes 262144
  50.1 0.0 copy-done
  50.1 0.0 copy-start.1
  50.1 0.7 %copy.16 = f32[512,128]{1,0:T(8,128)} copy(f32[512,128]{1,0:T(8,128)S(1)} %copy-done) | data formatting | bytes 524288
  50.8 0.3 copy-done.1
  51.1 0.7 %copy.17 = f32[256,128]{1,0:T(8,128)} copy(f32[256,128]{1,0:T(8,128)S(1)} %copy-done.1) | data formatting | bytes 262144
Async XLA Ops:
  48.4 1.6 %copy-start = (f32[512,128]{1,0:T(8,128)S(1)}, f32[512,128]{1,0:T(8,128)}, u32[]{:S(2)}) copy-start(f32[512,128]{1,0:T(8,128)} %get-tuple-element.7) | copy-start | bytes 786436
  50.1 1.0 %copy-start.1 = (f32[256,128]{1,0:T(8,128)S(1)}, f32[256,128]{1,0:T(8,128)}, u32[]{:S(2)}) copy-start(f32[256,128]{1,0:T(8,128)} %get-tuple-element.8) | copy-start | bytes 393220
